TPU v7x, 32 devices: a whole 2x2x4 slice. The times are simulated.
32 devices in a mesh: groups: 2 (over x), grid: 16 (over z, y, core).
Axes of the slice: x: 2, y: 2, z: 4, core: 2. Of those that a mesh axis runs over, the one named last changes fastest.
Arguments:
- source: bfloat16 [1536, 8192], P('groups', 'grid'), parts along dimension 0, may hold values from -6 to 6
- target: bfloat16 [1536, 8192], P('groups', 'grid'), parts along dimension 0, may hold values from -6 to 6
Outputs:
- cross_gram: float32 [16384, 8192], P(('groups', 'grid')), parts along dimension 0
- self_gram: float32 [16384, 8192], P(('groups', 'grid')), parts along dimension 0
There are 2 independent parts, one for each index of `groups`. A program takes and returns all parts, laid end to end along the dimension named above; each array names one. Nothing has to cross between parts.
All inputs are finite; a program needn't handle non-finite values.
Results may differ from a plain program's by a relative error of at most 0.0003.
Values may be sent and summed in bfloat16 or wider, within the bound.
A program may use at most 128 MiB of HBM per device.

v0:
```python
import jax
import jax.numpy as jnp
from jax import lax
from jax.sharding import PartitionSpec as P


def block_product(left, right):
    return lax.dot_general(
        left, right, (((0,), (0,)), ((), ())), preferred_element_type=jnp.float32
    )


def shards(source, target):
    tokens_here = source.shape[0]
    scale = 1.0 / tokens_here
    cross_acc = block_product(source, lax.all_gather(target, "grid", axis=1, tiled=True))
    self_acc = block_product(source, lax.all_gather(source, "grid", axis=1, tiled=True))
    return (cross_acc * scale, self_acc * scale)


def solution(mesh):
    in_specs = (P("groups", "grid"), P("groups", "grid"))
    out_specs = (P(("groups", "grid"), None), P(("groups", "grid"), None))
    return jax.shard_map(shards, mesh=mesh, in_specs=in_specs, out_specs=out_specs, check_vma=False)
```

profile of v0, /device:TPU:0, one launch (start us, length us, event | category | flops | bytes accessed | tf_op | source)
XLA Modules:
  0.0 243.3 jit_solution(18174780471694720995)
XLA Ops:
  7.2 0.0 all-gather.5.cloned.1.call-start
  7.2 0.7 all-gather.5.cloned.1.call-update
  7.9 0.0 all-gather.3.cloned.1.call-start
  7.9 0.7 all-gather.3.cloned.1.call-update
  8.6 0.0 copy-start
  8.7 108.2 %all-gather.5.cloned.1.call-done = bf16[768,8192]{1,0:T(8,128)(2,1)} async-done(((bf16[768,512]{1,0:T(8,128)(2,1)}), bf16[768,8192]{1,0:T(8,128)(2,1)}) %all-gather.5.cloned.1.call-update) | async-done | bytes 12582928 | tf_op jit(solution)/shard_map/all_gather | solution.py:17
  116.8 15.4 %convolution_multiply_fusion = f32[512,8192]{1,0:T(8,128)} fusion(bf16[768,512]{1,0:T(8,128)(2,1)} %param.2, bf16[768,8192]{1,0:T(8,128)(2,1)} %all-gather.5.cloned.1.call-done), kind=kOutput, calls=%fused_computation | convolution fusion | flops 6446645248 | bytes 30146560 | tf_op jit(solution)/shard_map/dot_general | solution.py:8
  132.2 88.9 %all-gather.3.cloned.1.call-done = bf16[768,8192]{1,0:T(8,128)(2,1)} async-done(((bf16[768,512]{1,0:T(8,128)(2,1)}), bf16[768,8192]{1,0:T(8,128)(2,1)}) %all-gather.3.cloned.1.call-update) | async-done | bytes 12582928 | tf_op jit(solution)/shard_map/all_gather | solution.py:16
  221.1 0.0 copy-done
  221.2 15.3 %convolution_multiply_fusion.1 = f32[512,8192]{1,0:T(8,128)} fusion(bf16[768,512]{1,0:T(8,128)(2,1)S(1)} %copy-done, bf16[768,8192]{1,0:T(8,128)(2,1)} %all-gather.3.cloned.1.call-done), kind=kOutput, calls=%fused_computation.1 | convolution fusion | flops 6446645248 | bytes 30146560 | tf_op jit(solution)/shard_map/dot_general | solution.py:8
Async XLA Ops:
  7.2 109.7 %all-gather.5.cloned.1.call-start = ((), (), s32[]{:S(2)}) async-start(), calls=%async_computation.1 | async-start | bytes 13369344 | tf_op jit(solution)/shard_map/all_gather | solution.py:17
  7.9 213.3 %all-gather.3.cloned.1.call-start = ((), (), s32[]{:S(2)}) async-start(), calls=%async_computation | async-start | bytes 13369344 | tf_op jit(solution)/shard_map/all_gather | solution.py:16
  8.6 212.5 %copy-start = (bf16[768,512]{1,0:T(8,128)(2,1)S(1)}, bf16[768,512]{1,0:T(8,128)(2,1)}, u32[]{:S(2)}) copy-start(bf16[768,512]{1,0:T(8,128)(2,1)} %param.2) | copy-start | bytes 2359300
Sparse Core Ops, SparseCore 0:
  10.2 106.6 all-gather.4
  119.0 102.1 all-gather.2
where the time goes:
time: 243 us
  waiting for transfers between devices  198 us (81%)
  matrix products  30.7 us (13%)
  between operations  14 us (6%)
    all_gather x1, waiting for transfers between devices, shards(): lax.all_gather(source, 'grid', axis=1, tiled=True)  108 us
    all_gather x1, waiting for transfers between devices, shards(): lax.all_gather(target, 'grid', axis=1, tiled=True)  88.9 us
    dot_general x2, matrix products, block_product(): lax.dot_general(left, right, (((0,), (0,)), ((), ())), preferred_element_...  30.7 us
  transfers between devices with their start and end apart: 2, of which 2 were waited for; matrix products, arithmetic and copies ran while one was open for 6% of the time, Pallas kernels for 0%

commit v1 on v0

v1 whole, which is shorter than its diff:
```python
import functools

import jax
import jax.numpy as jnp
from jax import lax
from jax.experimental import pallas as pl
from jax.experimental.pallas import tpu as pltpu
from jax.sharding import PartitionSpec as P

MESH = pl.DeviceIdType.MESH


def gather_kernel(Z, Y, PA, PB, s_ref, t_ref, g, local_sem, recv, crecv, zsend, zsendp, ysend, csend):
    K = PA + PB
    tokens, width = s_ref.shape
    R = 2 * tokens // K
    me = lax.axis_index("grid")
    c = me % 2
    y = (me // 2) % Y
    z = me // (2 * Y)

    def dev(zz, yy, cc):
        return (zz * Y + yy) * 2 + cc

    def rows(p):
        return pl.ds(pl.multiple_of(p * R, R), R)

    left, right = dev(z - 1, y, c), dev(z + 1, y, c)
    partner, sibling = dev(z, Y - 1 - y, c), dev(z, y, 1 - c)
    has_left, has_right = z > 0, z < Z - 1

    barrier = pltpu.get_barrier_semaphore()

    def greet(target):
        pl.semaphore_signal(barrier, inc=1, device_id={"grid": target}, device_id_type=MESH)

    @pl.when(has_left)
    def _():
        greet(left)

    @pl.when(has_right)
    def _():
        greet(right)

    if Y > 1:
        greet(partner)
    greet(sibling)
    pl.semaphore_wait(
        barrier, (2 if Y > 1 else 1) + has_left.astype(jnp.int32) + has_right.astype(jnp.int32)
    )

    def remote(src, dst, send, got, target):
        return pltpu.make_async_remote_copy(
            src_ref=src, dst_ref=dst, send_sem=send, recv_sem=got,
            device_id={"grid": target}, device_id_type=MESH,
        )

    def own(p):
        half = K // 2
        ref = s_ref if p < half else t_ref
        return ref.at[pl.ds((p % half) * R, R), :]

    order = list(range(PA, K)) + list(range(PA))
    if Y > 1:
        for p in order:
            remote(own(p), g.at[me, pl.ds(p * R, R), :], ysend.at[z], recv.at[z * Y + y, p], partner).start()

    @pl.when(has_right)
    def _():
        for p in range(K):
            remote(own(p), g.at[me, pl.ds(p * R, R), :], zsend.at[0, z], recv.at[z * Y + y, p], right).start()

    @pl.when(has_left)
    def _():
        for p in range(K):
            remote(own(p), g.at[me, pl.ds(p * R, R), :], zsend.at[1, z], recv.at[z * Y + y, p], left).start()

    locals_ = []
    for h, ref in enumerate((s_ref, t_ref)):
        dst = g.at[me, pl.ds(h * tokens, tokens), :]
        remote(ref, dst, csend.at[z * Y + y], crecv.at[z * Y + y], sibling).start()
        cp = pltpu.make_async_copy(ref, dst, local_sem.at[h])
        cp.start()
        locals_.append(cp)

    def wait_piece(zz, yy, p):
        at = g.at[dev(zz, yy, c), rows(p), :]
        remote(at, at, csend.at[zz * Y + yy], recv.at[zz * Y + yy, p], sibling).wait_recv()

    def send_piece(zz, yy, p, send, target):
        at = g.at[dev(zz, yy, c), rows(p), :]
        remote(at, at, send, recv.at[zz * Y + yy, p], target).start()

    def share_piece(zz, yy, p):
        at = g.at[dev(zz, yy, c), rows(p), :]
        remote(at, at, csend.at[zz * Y + yy], crecv.at[zz * Y + yy], sibling).start()

    per = K + (PB if Y > 1 else 0)
    n_left, n_right = z, Z - 1 - z
    least = jnp.minimum(n_left, n_right)

    def from_z(t, side):
        k = t // per + 1
        q = t % per
        zo = z - k if side == 0 else z + k
        there = zo >= 0 if side == 0 else zo <= Z - 1
        onward = has_right if side == 0 else has_left
        target = right if side == 0 else left

        @pl.when(there & (q < K))
        def _():
            wait_piece(zo, y, q)

            @pl.when(onward)
            def _():
                send_piece(zo, y, q, zsend.at[side, zo], target)

            if Y > 1:
                @pl.when(q < PA)
                def _():
                    send_piece(zo, y, q, ysend.at[zo], partner)

            share_piece(zo, y, q)

        if Y > 1 and PB > 0:
            @pl.when(there & (q >= K))
            def _():
                yo, p = Y - 1 - y, q - PB
                wait_piece(zo, yo, p)

                @pl.when(onward)
                def _():
                    send_piece(zo, yo, p, zsendp.at[side, zo], target)

                share_piece(zo, yo, p)

    def from_y(u):
        yo = Y - 1 - y

        @pl.when(u < PB)
        def _():
            p = PA + u
            wait_piece(z, yo, p)

            @pl.when(has_right)
            def _():
                send_piece(z, yo, p, zsendp.at[0, z], right)

            @pl.when(has_left)
            def _():
                send_piece(z, yo, p, zsendp.at[1, z], left)

            share_piece(z, yo, p)

        @pl.when((u >= PB) & (u < K))
        def _():
            p = u - PB
            wait_piece(z, yo, p)
            share_piece(z, yo, p)

        @pl.when(u >= K)
        def _():
            i = u - K
            both = i < 2 * PA * least
            i1 = i - 2 * PA * least
            pair = i // 2
            k = jnp.where(both, pair // PA, least + i1 // PA) + 1
            p = jnp.where(both, pair % PA, i1 % PA)
            go_left = jnp.where(both, i % 2, (n_left < n_right).astype(jnp.int32))
            zo = jnp.where(go_left == 1, z + k, z - k)
            wait_piece(zo, yo, p)
            share_piece(zo, yo, p)

    slots = per * (Z - 1)
    y_slots = K + PA * (Z - 1) if Y > 1 else 0

    @pl.loop(0, max(slots, y_slots))
    def _(t):
        if y_slots:
            @pl.when(t < y_slots)
            def _():
                from_y(t)
        from_z(t, 0)
        from_z(t, 1)

    for cp in locals_:
        cp.wait()

    @pl.loop(0, Z)
    def _(zo):
        for side in range(2):
            sent = (zo <= z) & has_right if side == 0 else (zo >= z) & has_left

            @pl.when(sent)
            def _():
                at = g.at[0]
                remote(at, at, zsend.at[side, zo], crecv.at[0], sibling).wait_send()
                if Y > 1 and PB > 0:
                    at = g.at[0, pl.ds(PA * R, PB * R), :]
                    remote(at, at, zsendp.at[side, zo], crecv.at[0], sibling).wait_send()

        if Y > 1:
            @pl.when(zo == z)
            def _():
                at = g.at[0]
                remote(at, at, ysend.at[zo], crecv.at[0], sibling).wait_send()

            @pl.when(zo != z)
            def _():
                at = g.at[0, pl.ds(0, PA * R), :]
                remote(at, at, ysend.at[zo], crecv.at[0], sibling).wait_send()

        for yo in range(Y):
            at = g.at[dev(zo, yo, 1 - c)]
            remote(at, at, csend.at[zo * Y + yo], crecv.at[zo * Y + yo], sibling).wait()


def gather(source, target, Z, Y):
    tokens, width = source.shape
    PA, PB = (10, 2) if Y > 1 else (4, 0)
    n = Z * Y * 2
    dma = pltpu.SemaphoreType.DMA
    return pl.pallas_call(
        functools.partial(gather_kernel, Z, Y, PA, PB),
        out_shape=jax.ShapeDtypeStruct((n, 2 * tokens, width), source.dtype),
        in_specs=[pl.BlockSpec(memory_space=pl.ANY)] * 2,
        out_specs=pl.BlockSpec(memory_space=pl.ANY),
        scratch_shapes=[
            dma((2,)),
            dma((Z * Y, PA + PB)),
            dma((Z * Y,)),
            dma((2, Z)),
            dma((2, Z)),
            dma((Z,)),
            dma((Z * Y,)),
        ],
        compiler_params=pltpu.CompilerParams(collective_id=0, has_side_effects=True),
    )(source, target)


def product_kernel(scale, s_ref, g_ref, cross_ref, self_ref, st):
    tokens, width = s_ref.shape
    per = g_ref.shape[0]

    @pl.when(pl.program_id(0) == 0)
    def _():
        st[...] = s_ref[...].T

    for j in range(per):
        at = slice(j * width, (j + 1) * width)
        self_ref[:, at] = jnp.dot(st[...], g_ref[j, :tokens, :], preferred_element_type=jnp.float32) * scale
        cross_ref[:, at] = jnp.dot(st[...], g_ref[j, tokens:, :], preferred_element_type=jnp.float32) * scale


def products(source, gathered):
    tokens, width = source.shape
    n = gathered.shape[0]
    per = max(1, 512 // width)
    out = jax.ShapeDtypeStruct((width, n * width), jnp.float32)
    out_spec = pl.BlockSpec((width, per * width), lambda i: (0, i))
    return pl.pallas_call(
        functools.partial(product_kernel, 1.0 / tokens),
        grid=(n // per,),
        out_shape=(out, out),
        in_specs=[
            pl.BlockSpec((tokens, width), lambda i: (0, 0)),
            pl.BlockSpec((per, 2 * tokens, width), lambda i: (i, 0, 0)),
        ],
        out_specs=(out_spec, out_spec),
        scratch_shapes=[pltpu.VMEM((width, tokens), source.dtype)],
        compiler_params=pltpu.CompilerParams(
            dimension_semantics=("arbitrary",), vmem_limit_bytes=32 << 20
        ),
        cost_estimate=pl.CostEstimate(
            flops=4 * width * width * n * tokens,
            bytes_accessed=n * width * (4 * tokens + 8 * width),
            transcendentals=0,
        ),
    )(source, gathered)


def solution(mesh):
    n = mesh.shape["grid"]
    Y = max(1, 4 // mesh.shape["groups"])
    Z = n // (2 * Y)

    def shards(source, target):
        gathered = gather(source, target, Z, Y)
        return products(source, gathered)

    specs = (P("groups", "grid"), P("groups", "grid"))
    out_specs = (P(("groups", "grid"), None), P(("groups", "grid"), None))
    return jax.shard_map(shards, mesh=mesh, in_specs=specs, out_specs=out_specs, check_vma=False)
```

time: 243 us -> 155 us (0.64)
  waiting for transfers between devices: 198 us -> 0 us
  Pallas kernels: 0 us -> 154 us
  matrix products: 30.7 us -> 0 us
  between operations: 14 us -> 0.65 us
    all_gather x2 -> x0, waiting for transfers between devices: 197 us -> none  [the longest x1 108 us: shards(): lax.all_gather(source, 'grid', axis=1, tiled=True)]
    pallas_call x0 -> x2, Pallas kernels: none -> 154 us  [the longest x1 126 us: gather(): pl.pallas_call(functools.partial(gather_kernel, Z, Y, PA, PB), out_shape=...]
    dot_general x2 -> x0, matrix products: 30.7 us -> none  [block_product(): lax.dot_general(left, right, (((0,), (0,)), ((), ())), preferred_element_...]
  transfers between devices with their start and end apart: 2 -> 0, of which waited for: 2 -> 0; matrix products, arithmetic and copies ran while one was open for 6% -> 0% of each run, Pallas kernels for 0% -> 0%
where the time goes in v1:
time: 155 us; the launch traced here: 154 us
  Pallas kernels  154 us (99%)
    pallas_call x1, Pallas kernels, gather(): pl.pallas_call(functools.partial(gather_kernel, Z, Y, PA, PB), out_shape=...  126 us
    pallas_call x1, Pallas kernels, products(): pl.pallas_call(functools.partial(product_kernel, 1.0 / tokens), grid=(n /...  27.8 us

profile of v1, /device:TPU:0, one launch (start us, length us, event | category | flops | bytes accessed | tf_op | source)
XLA Modules:
  0.0 154.5 jit_solution(10276551566328285823)
XLA Ops:
  0.6 0.0 copy-start
  0.6 126.0 %shard_map.41.g_ref = bf16[16,1536,512]{2,1,0:T(8,128)(2,1)} custom-call(bf16[768,512]{1,0:T(8,128)(2,1)} %s_ref.3, bf16[768,512]{1,0:T(8,128)(2,1)} %t_ref.1), custom_call_target="tpu_custom_call" | custom-call | tf_op jit(solution)/shard_map/pallas_call | solution.py:223
  126.6 0.0 copy-done
  126.6 27.8 %shard_map.42 = (f32[512,8192]{1,0:T(8,128)}, f32[512,8192]{1,0:T(8,128)}) custom-call(bf16[768,512]{1,0:T(8,128)(2,1)S(1)} %copy-done, bf16[16,1536,512]{2,1,0:T(8,128)(2,1)} %shard_map.41.g_ref), custom_call_target="tpu_custom_call" | custom-call | flops 12884901888 | bytes 58720256 | tf_op jit(solution)/shard_map/pallas_call | solution.py:261
Async XLA Ops:
  0.6 126.0 %copy-start = (bf16[768,512]{1,0:T(8,128)(2,1)S(1)}, bf16[768,512]{1,0:T(8,128)(2,1)}, u32[]{:S(2)}) copy-start(bf16[768,512]{1,0:T(8,128)(2,1)} %s_ref.3) | copy-start | bytes 2359300

commit v2 on v1

--- a/solution.py
+++ b/solution.py
@@ -10,7 +10,7 @@
 MESH = pl.DeviceIdType.MESH
 
 
-def gather_kernel(Z, Y, PA, PB, s_ref, t_ref, g, local_sem, recv, crecv, zsend, zsendp, ysend, csend):
+def gather_kernel(Z, Y, PA, PB, s_ref, t_ref, out, g, st, local_sem, recv, crecv, zsend, zsendp, ysend, csend):
     K = PA + PB
     tokens, width = s_ref.shape
     R = 2 * tokens // K
@@ -78,7 +78,7 @@
     locals_ = []
     for h, ref in enumerate((s_ref, t_ref)):
         dst = g.at[me, pl.ds(h * tokens, tokens), :]
-        remote(ref, dst, csend.at[z * Y + y], crecv.at[z * Y + y], sibling).start()
+        remote(ref, dst, csend.at[z * Y + y], crecv.at[z * Y + y, h], sibling).start()
         cp = pltpu.make_async_copy(ref, dst, local_sem.at[h])
         cp.start()
         locals_.append(cp)
@@ -93,9 +93,41 @@
 
     def share_piece(zz, yy, p):
         at = g.at[dev(zz, yy, c), rows(p), :]
-        remote(at, at, csend.at[zz * Y + yy], crecv.at[zz * Y + yy], sibling).start()
+        half = jnp.int32(p >= K // 2)
+        remote(at, at, csend.at[zz * Y + yy], crecv.at[zz * Y + yy, half], sibling).start()
+
+    for cp in locals_:
+        cp.wait()
+    st[...] = g[me, pl.ds(0, tokens), :].T
+
+    def multiply(zz, yy, first, count):
+        @pl.loop(first, first + count)
+        def _(kind):
+            half, other = kind // 2, kind % 2
+            block = dev(zz, yy, jnp.where(other == 1, 1 - c, c))
+            at = g.at[block, pl.ds(pl.multiple_of(half * tokens, tokens), tokens), :]
+
+            @pl.when(other == 1)
+            def _():
+                remote(at, at, csend.at[0], crecv.at[zz * Y + yy, half], sibling).wait_recv()
+
+            out[half, :, pl.ds(pl.multiple_of(block * width, width), width)] = (
+                jnp.dot(st[...], at[...], preferred_element_type=jnp.float32) * (1.0 / tokens)
+            )
 
     per = K + (PB if Y > 1 else 0)
+
+    def picks(q, table):
+        first, count = jnp.int32(0), jnp.int32(0)
+        for when, a, b in table:
+            first, count = jnp.where(q == when, a, first), jnp.where(q == when, b, count)
+        return first, count
+
+    if Y > 1:
+        z_table = ((K // 2, 0, 1), (K // 2 + 2, 1, 1), (K, 2, 1), (per - 1, 3, 1))
+    else:
+        z_table = ((K // 2, 0, 1), (K - 1, 1, 3))
+    y_table = ((K // 2, 0, 1), (K // 2 + 2, 1, 1), (PA - 1, 2, 2))
     n_left, n_right = z, Z - 1 - z
     least = jnp.minimum(n_left, n_right)
 
@@ -134,6 +166,9 @@
 
                 share_piece(zo, yo, p)
 
+        first, count = picks(q, z_table)
+        return zo, y, first, jnp.where(there, count, 0)
+
     def from_y(u):
         yo = Y - 1 - y
 
@@ -152,39 +187,37 @@
 
             share_piece(z, yo, p)
 
-        @pl.when((u >= PB) & (u < K))
+        i = u - K
+        both = i < 2 * PA * least
+        i1 = i - 2 * PA * least
+        pair = i // 2
+        k = jnp.where(both, pair // PA, least + i1 // PA) + 1
+        go_left = jnp.where(both, i % 2, (n_left < n_right).astype(jnp.int32))
+        far = jnp.where(go_left == 1, z + k, z - k)
+        direct = u < K
+        zo = jnp.where(direct, z, far)
+        p = jnp.where(direct, u - PB, jnp.where(both, pair % PA, i1 % PA))
+
+        @pl.when((u >= PB) & (u < y_slots))
         def _():
-            p = u - PB
-            wait_piece(z, yo, p)
-            share_piece(z, yo, p)
-
-        @pl.when(u >= K)
-        def _():
-            i = u - K
-            both = i < 2 * PA * least
-            i1 = i - 2 * PA * least
-            pair = i // 2
-            k = jnp.where(both, pair // PA, least + i1 // PA) + 1
-            p = jnp.where(both, pair % PA, i1 % PA)
-            go_left = jnp.where(both, i % 2, (n_left < n_right).astype(jnp.int32))
-            zo = jnp.where(go_left == 1, z + k, z - k)
             wait_piece(zo, yo, p)
             share_piece(zo, yo, p)
 
+        first, count = picks(p, y_table)
+        return zo, yo, first, jnp.where((u >= PB) & (u < y_slots), count, 0)
+
     slots = per * (Z - 1)
     y_slots = K + PA * (Z - 1) if Y > 1 else 0
 
+    multiply(z, y, 0, 4)
+
     @pl.loop(0, max(slots, y_slots))
     def _(t):
+        work = [from_z(t, 0), from_z(t, 1)]
         if y_slots:
-            @pl.when(t < y_slots)
-            def _():
-                from_y(t)
-        from_z(t, 0)
-        from_z(t, 1)
-
-    for cp in locals_:
-        cp.wait()
+            work.append(from_y(t))
+        for todo in work:
+            multiply(*todo)
 
     @pl.loop(0, Z)
     def _(zo):
@@ -194,89 +227,89 @@
             @pl.when(sent)
             def _():
                 at = g.at[0]
-                remote(at, at, zsend.at[side, zo], crecv.at[0], sibling).wait_send()
+                remote(at, at, zsend.at[side, zo], crecv.at[0, 0], sibling).wait_send()
                 if Y > 1 and PB > 0:
                     at = g.at[0, pl.ds(PA * R, PB * R), :]
-                    remote(at, at, zsendp.at[side, zo], crecv.at[0], sibling).wait_send()
+                    remote(at, at, zsendp.at[side, zo], crecv.at[0, 0], sibling).wait_send()
 
         if Y > 1:
             @pl.when(zo == z)
             def _():
                 at = g.at[0]
-                remote(at, at, ysend.at[zo], crecv.at[0], sibling).wait_send()
+                remote(at, at, ysend.at[zo], crecv.at[0, 0], sibling).wait_send()
 
             @pl.when(zo != z)
             def _():
                 at = g.at[0, pl.ds(0, PA * R), :]
-                remote(at, at, ysend.at[zo], crecv.at[0], sibling).wait_send()
+                remote(at, at, ysend.at[zo], crecv.at[0, 0], sibling).wait_send()
 
         for yo in range(Y):
-            at = g.at[dev(zo, yo, 1 - c)]
-            remote(at, at, csend.at[zo * Y + yo], crecv.at[zo * Y + yo], sibling).wait()
-
-
-def gather(source, target, Z, Y):
+            at = g.at[0]
+            remote(at, at, csend.at[zo * Y + yo], crecv.at[0, 0], sibling).wait_send()
+
+
+def gather_products(source, target, Z, Y):
     tokens, width = source.shape
     PA, PB = (10, 2) if Y > 1 else (4, 0)
     n = Z * Y * 2
     dma = pltpu.SemaphoreType.DMA
     return pl.pallas_call(
         functools.partial(gather_kernel, Z, Y, PA, PB),
-        out_shape=jax.ShapeDtypeStruct((n, 2 * tokens, width), source.dtype),
+        out_shape=pltpu.VMEM((2, width, n * width), jnp.float32),
         in_specs=[pl.BlockSpec(memory_space=pl.ANY)] * 2,
-        out_specs=pl.BlockSpec(memory_space=pl.ANY),
+        out_specs=pl.BlockSpec(memory_space=pltpu.VMEM),
         scratch_shapes=[
+            pltpu.VMEM((n, 2 * tokens, width), source.dtype),
+            pltpu.VMEM((width, tokens), source.dtype),
             dma((2,)),
             dma((Z * Y, PA + PB)),
-            dma((Z * Y,)),
+            dma((Z * Y, 2)),
             dma((2, Z)),
             dma((2, Z)),
             dma((Z,)),
             dma((Z * Y,)),
         ],
-        compiler_params=pltpu.CompilerParams(collective_id=0, has_side_effects=True),
-    )(source, target)
-
-
-def product_kernel(scale, s_ref, g_ref, cross_ref, self_ref, st):
-    tokens, width = s_ref.shape
-    per = g_ref.shape[0]
-
-    @pl.when(pl.program_id(0) == 0)
-    def _():
-        st[...] = s_ref[...].T
-
-    for j in range(per):
-        at = slice(j * width, (j + 1) * width)
-        self_ref[:, at] = jnp.dot(st[...], g_ref[j, :tokens, :], preferred_element_type=jnp.float32) * scale
-        cross_ref[:, at] = jnp.dot(st[...], g_ref[j, tokens:, :], preferred_element_type=jnp.float32) * scale
-
-
-def products(source, gathered):
-    tokens, width = source.shape
-    n = gathered.shape[0]
-    per = max(1, 512 // width)
-    out = jax.ShapeDtypeStruct((width, n * width), jnp.float32)
-    out_spec = pl.BlockSpec((width, per * width), lambda i: (0, i))
-    return pl.pallas_call(
-        functools.partial(product_kernel, 1.0 / tokens),
-        grid=(n // per,),
-        out_shape=(out, out),
-        in_specs=[
-            pl.BlockSpec((tokens, width), lambda i: (0, 0)),
-            pl.BlockSpec((per, 2 * tokens, width), lambda i: (i, 0, 0)),
-        ],
-        out_specs=(out_spec, out_spec),
-        scratch_shapes=[pltpu.VMEM((width, tokens), source.dtype)],
         compiler_params=pltpu.CompilerParams(
-            dimension_semantics=("arbitrary",), vmem_limit_bytes=32 << 20
+            collective_id=0, has_side_effects=True, vmem_limit_bytes=28 << 20
         ),
         cost_estimate=pl.CostEstimate(
             flops=4 * width * width * n * tokens,
             bytes_accessed=n * width * (4 * tokens + 8 * width),
             transcendentals=0,
         ),
-    )(source, gathered)
+    )(source, target)
+
+
+def store_kernel(products, cross_ref, self_ref, sem):
+    width = products.shape[1]
+    parts = sem.shape[1]
+    rows = width // parts
+    copies = []
+    for part in range(parts):
+        at = pl.ds(part * rows, rows)
+        for half, ref in enumerate((self_ref, cross_ref)):
+            copies.append(
+                pltpu.make_async_copy(products.at[half, at, :], ref.at[at, :], sem.at[half, part])
+            )
+            copies[-1].start()
+    for copy in copies:
+        copy.wait()
+
+
+def store(products):
+    _, width, columns = products.shape
+    out = jax.ShapeDtypeStruct((width, columns), jnp.float32)
+    return pl.pallas_call(
+        store_kernel,
+        out_shape=(out, out),
+        in_specs=[pl.BlockSpec(memory_space=pl.ANY)],
+        out_specs=(pl.BlockSpec(memory_space=pl.ANY),) * 2,
+        scratch_shapes=[pltpu.SemaphoreType.DMA((2, 8))],
+        compiler_params=pltpu.CompilerParams(vmem_limit_bytes=1 << 20),
+        cost_estimate=pl.CostEstimate(
+            flops=0, bytes_accessed=8 * width * columns, transcendentals=0
+        ),
+    )(pltpu.with_memory_space_constraint(products, pltpu.VMEM))
 
 
 def solution(mesh):
@@ -285,8 +318,7 @@
     Z = n // (2 * Y)
 
     def shards(source, target):
-        gathered = gather(source, target, Z, Y)
-        return products(source, gathered)
+        return store(gather_products(source, target, Z, Y))
 
     specs = (P("groups", "grid"), P("groups", "grid"))
     out_specs = (P(("groups", "grid"), None), P(("groups", "grid"), None))

time: 155 us -> 138 us (0.89)
  Pallas kernels: 154 us -> 137 us
    pallas_call x2, Pallas kernels: 154 us -> 137 us  [the longest x1 126 us: gather_products(): pl.pallas_call(functools.partial(gather_kernel, Z, Y, PA, PB), out_shape=...]
where the time goes in v2:
time: 138 us
  Pallas kernels  137 us (99%)
    pallas_call x1, Pallas kernels, gather_products(): pl.pallas_call(functools.partial(gather_kernel, Z, Y, PA, PB), out_shape=...  126 us
    pallas_call x1, Pallas kernels, store(): pl.pallas_call(store_kernel, out_shape=(out, out), in_specs=[pl.BlockSpec...  11 us

profile of v2, /device:TPU:0, one launch (start us, length us, event | category | flops | bytes accessed | tf_op | source)
XLA Modules:
  0.0 138.1 jit_solution(3326370868258364038)
XLA Ops:
  0.6 126.4 %shard_map.41.products = f32[2,512,8192]{2,1,0:T(8,128)S(1)} custom-call(bf16[768,512]{1,0:T(8,128)(2,1)} %s_ref.1, bf16[768,512]{1,0:T(8,128)(2,1)} %t_ref.1), custom_call_target="tpu_custom_call" | custom-call | flops 12884901888 | bytes 58720256 | tf_op jit(solution)/shard_map/pallas_call | solution.py:256
  127.0 11.0 %shard_map.42 = (f32[512,8192]{1,0:T(8,128)}, f32[512,8192]{1,0:T(8,128)}) custom-call(f32[2,512,8192]{2,1,0:T(8,128)S(1)} %shard_map.41.products), custom_call_target="tpu_custom_call" | custom-call | bytes 33554432 | tf_op jit(solution)/shard_map/pallas_call | solution.py:302

commit v3 on v2

--- a/solution.py
+++ b/solution.py
@@ -61,10 +61,6 @@
         return ref.at[pl.ds((p % half) * R, R), :]
 
     order = list(range(PA, K)) + list(range(PA))
-    if Y > 1:
-        for p in order:
-            remote(own(p), g.at[me, pl.ds(p * R, R), :], ysend.at[z], recv.at[z * Y + y, p], partner).start()
-
     @pl.when(has_right)
     def _():
         for p in range(K):
@@ -74,6 +70,10 @@
     def _():
         for p in range(K):
             remote(own(p), g.at[me, pl.ds(p * R, R), :], zsend.at[1, z], recv.at[z * Y + y, p], left).start()
+
+    if Y > 1:
+        for p in order:
+            remote(own(p), g.at[me, pl.ds(p * R, R), :], ysend.at[z], recv.at[z * Y + y, p], partner).start()
 
     locals_ = []
     for h, ref in enumerate((s_ref, t_ref)):

time: 138 us -> 138 us (level)
  no operation moved by 1% of the time
where the time goes in v3:
time: 138 us
  Pallas kernels  137 us (99%)
    pallas_call x1, Pallas kernels, gather_products(): pl.pallas_call(functools.partial(gather_kernel, Z, Y, PA, PB), out_shape=...  126 us
    pallas_call x1, Pallas kernels, store(): pl.pallas_call(store_kernel, out_shape=(out, out), in_specs=[pl.BlockSpec...  11 us

profile of v3, /device:TPU:0, one launch (start us, length us, event | category | flops | bytes accessed | tf_op | source)
XLA Modules:
  0.0 138.0 jit_solution(15060543729959758815)
XLA Ops:
  0.6 126.4 %shard_map.41.products = f32[2,512,8192]{2,1,0:T(8,128)S(1)} custom-call(bf16[768,512]{1,0:T(8,128)(2,1)} %s_ref.1, bf16[768,512]{1,0:T(8,128)(2,1)} %t_ref.1), custom_call_target="tpu_custom_call" | custom-call | flops 12884901888 | bytes 58720256 | tf_op jit(solution)/shard_map/pallas_call | solution.py:256
  127.0 11.0 %shard_map.42 = (f32[512,8192]{1,0:T(8,128)}, f32[512,8192]{1,0:T(8,128)}) custom-call(f32[2,512,8192]{2,1,0:T(8,128)S(1)} %shard_map.41.products), custom_call_target="tpu_custom_call" | custom-call | bytes 33554432 | tf_op jit(solution)/shard_map/pallas_call | solution.py:302
